TPU v7x, 256 devices: a whole 4x4x8 slice. The times are simulated.
256 devices in a mesh: ep: 8 (over y, core), seq: 32 (over z, x).
Axes of the slice: x: 4, y: 4, z: 8, core: 2. Of those that a mesh axis runs over, the one named last changes fastest.
Arguments:
- frames: bfloat16 [8, 22528, 512], P('ep', 'seq'), may hold values from -6 to 6
- lengths: int32 [8], P('ep'), may hold values from 11264 to 22528
- w_in: bfloat16 [512, 1024], replicated, may hold values from -0.25 to 0.25
- kernel: float32 [31, 512], replicated, may hold values from -1 to 1
- w_out: bfloat16 [512, 512], replicated, may hold values from -0.25 to 0.25
- pool_query: bfloat16 [8, 512], replicated, may hold values from -600 to 600
- w_value: bfloat16 [512, 512], replicated, may hold values from -0.25 to 0.25
- text_emb: bfloat16 [256, 512], replicated, may hold values from -6 to 6
- teacher: float32 [8, 256], P('ep'), may hold values from -6 to 6
Outputs:
- loss: float32 [], replicated
- grad_in: float32 [512, 1024], P('seq', 'ep')
- grad_out: float32 [512, 512], P('seq', 'ep')
- grad_kernel: float32 [31, 512], replicated
- grad_query: float32 [8, 512], replicated
- grad_value: float32 [512, 512], replicated
All inputs are finite; a program needn't handle non-finite values.
Results may differ from a plain program's by a relative error of at most 0.03.
Values may be sent and summed in bfloat16 or wider, within the bound.
No kernel may reach another device: no remote copies, remote signals or barrier semaphores. Data moves between devices by JAX's collectives and lax.ppermute only.
A program may use at most 64 MiB of HBM per device.

v0:
```python
import jax
import jax.numpy as jnp
from jax import lax
from jax.sharding import PartitionSpec as P


def padded_2(block, sides, width):
    for axis, dim in sides:
        count = lax.axis_size(axis)
        forward = [(i, i + 1) for i in range(count - 1)]
        backward = [(target, source) for source, target in forward]
        low = lax.ppermute(
            lax.slice_in_dim(block, block.shape[dim] - width, None, axis=dim), axis, forward
        )
        high = lax.ppermute(lax.slice_in_dim(block, 0, width, axis=dim), axis, backward)
        block = jnp.concatenate([low, block, high], axis=dim)
    return block


def shards(frames, lengths, w_in, kernel, w_out, pool_query, w_value, text_emb, teacher):
    hi = lax.Precision.HIGHEST
    n_epis, n_rows, width = frames.shape
    n_taps = kernel.shape[0]
    rim = n_taps // 2
    n_heads = pool_query.shape[0]
    head_dim = width // n_heads
    n_cands = text_emb.shape[0]
    root_width = jnp.sqrt(jnp.float32(width))
    offset = lax.axis_index("seq") * n_rows
    positions = offset + jnp.arange(n_rows, dtype=jnp.int32)
    valid = (positions[None, :] < lengths[:, None]).astype(jnp.float32)[..., None]
    xf = frames.astype(jnp.float32)
    mean_val = jnp.mean(xf, axis=-1, keepdims=True)
    var_val = jnp.mean((xf - mean_val) ** 2, axis=-1, keepdims=True)
    normed = ((xf - mean_val) * lax.rsqrt(var_val + 1e-05)).astype(jnp.bfloat16)
    mixed = jnp.einsum("esd,df->esf", normed, w_in, preferred_element_type=jnp.float32)
    sig = jax.nn.sigmoid(mixed[..., width:])
    glu = (mixed[..., :width] * sig * valid).astype(jnp.bfloat16)
    padded = padded_2(glu, (("seq", 1),), rim)
    conv = jnp.zeros((n_epis, n_rows, width), jnp.float32)
    for k in range(n_taps):
        conv = conv + kernel[k] * padded[:, k : k + n_rows].astype(jnp.float32)
    sconv = jax.nn.sigmoid(conv)
    act = (conv * sconv).astype(jnp.bfloat16)
    resid = xf + jnp.einsum("esd,df->esf", act, w_out, preferred_element_type=jnp.float32)
    queries = pool_query.astype(jnp.float32)
    scores = jnp.einsum("esd,hd->esh", resid, queries, precision=hi) / root_width
    masked = jnp.where(valid > 0, scores, -1e30)
    top = lax.pmax(jnp.max(masked, axis=1), "seq")
    expo = jnp.where(valid > 0, jnp.exp(masked - top[:, None]), 0.0)
    vec_here = jnp.einsum("esh,esd->ehd", expo, resid, precision=hi)
    total, vec = lax.psum((jnp.sum(expo, axis=1), vec_here), "seq")
    probs = jnp.where(valid > 0, jnp.exp(masked - top[:, None]), 0.0) / total[:, None]
    vbar = vec / total[..., None]
    wvals = w_value.astype(jnp.float32).reshape(width, n_heads, head_dim)
    pooled = jnp.einsum("ehd,dhk->ehk", vbar, wvals, precision=hi).reshape(n_epis, width)
    rms = jnp.sqrt(jnp.mean(pooled * pooled, axis=-1, keepdims=True) + 1e-06)
    emb = pooled / rms
    texts = text_emb.astype(jnp.float32)
    score = jnp.einsum("ed,cd->ec", emb, texts, precision=hi) / root_width
    diff = score - teacher
    loss_here = jnp.sum(diff * diff) / n_cands
    dscore = 2.0 * diff / n_cands
    demb = jnp.einsum("ec,cd->ed", dscore, texts, precision=hi) / root_width
    dpooled = (demb - emb * jnp.mean(demb * emb, axis=-1, keepdims=True)) / rms
    dp3 = dpooled.reshape(n_epis, n_heads, head_dim)
    value_here = jnp.einsum("ehd,ehk->dhk", vbar, dp3, precision=hi).reshape(width, width)
    dvbar = jnp.einsum("dhk,ehk->ehd", wvals, dp3, precision=hi)
    proj = jnp.einsum("esd,ehd->esh", resid, dvbar, precision=hi)
    centre = jnp.sum(dvbar * vbar, axis=-1)
    dscores = probs * (proj - centre[:, None])
    query_here = jnp.einsum("esh,esd->hd", dscores, resid, precision=hi) / root_width
    dresid = (
        jnp.einsum("esh,ehd->esd", probs, dvbar, precision=hi)
        + jnp.einsum("esh,hd->esd", dscores, queries, precision=hi) / root_width
    ).astype(jnp.bfloat16)
    out_here = jnp.einsum("esd,esf->df", act, dresid, preferred_element_type=jnp.float32)
    dact = jnp.einsum("esf,df->esd", dresid, w_out, preferred_element_type=jnp.float32)
    dconv = (dact * sconv * (1.0 + conv * (1.0 - sconv))).astype(jnp.bfloat16)
    dconv_f = dconv.astype(jnp.float32)
    dpad = padded_2(dconv, (("seq", 1),), rim)
    dglu = jnp.zeros((n_epis, n_rows, width), jnp.float32)
    taps = []
    for k in range(n_taps):
        dglu = dglu + kernel[k] * dpad[:, 2 * rim - k : 2 * rim - k + n_rows].astype(jnp.float32)
        taps.append(jnp.sum(padded[:, k : k + n_rows].astype(jnp.float32) * dconv_f, axis=(0, 1)))
    kernel_here = jnp.stack(taps)
    dglu = dglu * valid
    dmixed = jnp.concatenate(
        [dglu * sig, dglu * mixed[..., :width] * sig * (1.0 - sig)], axis=-1
    ).astype(jnp.bfloat16)
    in_here = jnp.einsum("esd,esf->df", normed, dmixed, preferred_element_type=jnp.float32)
    rows_in, rows_out = (
        lax.psum_scatter(
            in_here.astype(jnp.bfloat16), "seq", scatter_dimension=0, tiled=True
        ).astype(jnp.float32),
        lax.psum_scatter(
            out_here.astype(jnp.bfloat16), "seq", scatter_dimension=0, tiled=True
        ).astype(jnp.float32),
    )
    grad_in, grad_out = (
        lax.psum_scatter(
            rows_in.astype(jnp.bfloat16), "ep", scatter_dimension=1, tiled=True
        ).astype(jnp.float32),
        lax.psum_scatter(
            rows_out.astype(jnp.bfloat16), "ep", scatter_dimension=1, tiled=True
        ).astype(jnp.float32),
    )
    grad_kernel, grad_query = lax.psum((kernel_here, query_here), ("ep", "seq"))
    grad_value, loss = (
        lax.psum(value_here.astype(jnp.bfloat16), "ep").astype(jnp.float32),
        lax.psum(loss_here.astype(jnp.bfloat16), "ep").astype(jnp.float32),
    )
    return (loss, grad_in, grad_out, grad_kernel, grad_query, grad_value)


def solution(mesh):
    return jax.shard_map(
        shards,
        mesh=mesh,
        in_specs=(P("ep", "seq", None), P("ep"), P(), P(), P(), P(), P(), P(), P("ep", None)),
        out_specs=(P(), P("seq", "ep"), P("seq", "ep"), P(), P(), P()),
        check_vma=False,
    )
```

profile of v0, /device:TPU:1, one launch (start us, length us, event | category | flops | bytes accessed | tf_op | source)
XLA Modules:
  0.0 1106.2 jit_solution(10548095060268716896)
XLA Ops:
  8.0 1.3 convert_reduce_fusion
  9.3 1.5 fusion.5
  10.8 0.6 copy-done.88
  11.4 1.0 convolution_bitcast_fusion
  12.8 1.1 copy-done.3
  14.0 3.9 collective-permute-start
  17.9 1.3 collective-permute-start.1
  19.6 1.0 copy.20
  20.6 1.8 collective-permute-done.1
  22.6 9.4 fusion.36
  32.1 0.6 fusion.37
  33.2 0.9 fusion.189
  34.1 62.9 %pmax.7 = f32[8]{0:T(128)S(1)} all-reduce(f32[8]{0:T(128)S(1)} %get-tuple-element.101), channel_id=1, replica_groups=mesh['ep'=8,'seq'=32] {'seq'}, use_global_device_ids=true, to_apply=%region_3.4 | all-reduce | flops 8 | bytes 64 | tf_op jit(solution)/shard_map/pmax | solution.py:49
  97.0 0.7 fusion.164
  97.7 0.8 convolution_bitcast_fusion.3
  98.5 111.0 %all-reduce.1 = (f32[1,8,512]{2,1,0:T(8,128)}, f32[8]{0:T(128)S(1)}) all-reduce(f32[1,8,512]{2,1,0:T(8,128)S(1)} %convolution_bitcast_fusion.3, f32[8]{0:T(128)} %fusion.164), channel_id=1, replica_groups=mesh['ep'=8,'seq'=32] {'seq'}, use_global_device_ids=true, to_apply=%region_4.5 | all-reduce | flops 4104 | bytes 32832 | tf_op jit(solution)/shard_map/psum | solution.py:52
  209.5 0.9 fusion.180
  210.4 1.5 fusion.161
  211.9 0.6 multiply_reduce_fusion
  213.3 0.7 broadcast_divide_fusion.1
  213.9 0.7 div.113
  214.6 0.7 reshape.298
  215.3 1.0 fusion.190
  216.3 0.9 fusion.171
  217.2 1.3 multiply_reduce_fusion.1
  219.1 0.7 subtract_divide_fusion
  219.9 1.4 fusion.191
  221.3 0.9 fusion.181
  222.1 2.1 fusion.159
  224.3 2.0 fusion.94
  226.3 0.8 fusion.93
  227.1 0.5 copy-done.9
  227.7 2.1 fusion.67
  229.9 0.9 copy-done.1
  230.8 1.3 collective-permute-start.2
  232.4 4.2 collective-permute-start.3
  236.5 1.4 convolution_convert_fusion.1
  238.4 25.7 %fusion.96 = (bf16[704,512]{1,0:T(8,128)(2,1)S(1)}, f32[1,704,512]{2,1,0:T(8,128)S(1)}) fusion(f32[1,704,1024]{2,1,0:T(8,128)} %copy-done.3, f32[704]{0:T(1024)S(1)} %copy-done.15, bf16[1,704,512]{2,1,0:T(8,128)(2,1)} %copy-done.1, bf16[1,15,512]{2,1,0:T(8,128)(2,1)S(1)} %collective-permute-done.3, f32[512]{0:T(512)S(1)} %bitcast.173, f32[512]{0:T(512)S(1)} %bitcast.175, ...), kind=kLoop, calls=%fused_computation.235 | loop fusion | flops 67764224 | bytes 4422400 | tf_op jit(solution)/shard_map/concatenate | solution.py:89
  264.1 0.6 fusion.97
  265.2 2.1 convolution_convert_fusion
  267.5 1.0 multiply_convert_fusion.4
  268.5 2.5 fusion.82
  271.1 1.7 fusion.84
  272.8 1.5 fusion.83
  274.3 216.4 %reduce-scatter.11.cloned.1.call-done = bf16[16,512]{1,0:T(8,128)(2,1)} async-done(((bf16[512,512]{1,0:T(8,128)(2,1)}), bf16[16,512]{1,0:T(8,128)(2,1)}) %reduce-scatter.11.cloned.1.call-update) | async-done | bytes 16400 | tf_op jit(solution)/shard_map/reduce_scatter | solution.py:97
  490.6 1.5 copy.28
  492.2 2.2 fusion.68
  494.4 213.8 %reduce-scatter.9.cloned.1.call-done = bf16[16,1024]{1,0:T(8,128)(2,1)} async-done(((bf16[512,1024]{1,0:T(8,128)(2,1)}), bf16[16,1024]{1,0:T(8,128)(2,1)}) %reduce-scatter.9.cloned.1.call-update) | async-done | bytes 32784 | tf_op jit(solution)/shard_map/reduce_scatter | solution.py:94
  708.2 1.6 copy.26
  709.9 1.4 convolution_multiply_fusion.2
  711.3 2.5 stack.127
  713.9 0.6 multiply_reduce_fusion.2
  715.1 18.4 %psum.44 = bf16[]{:T(256)} all-reduce(bf16[]{:T(256)S(6)} %div.117), channel_id=1, replica_groups=mesh['ep'=8,'seq'=32] {'ep'}, use_global_device_ids=true, to_apply=%region_9.10 | all-reduce | flops 1 | bytes 4 | tf_op jit(solution)/shard_map/psum | solution.py:112
  734.2 44.1 %all-reduce.5.cloned.1.call-done = bf16[512,512]{0,1:T(8,128)(2,1)} async-done(((bf16[512,512]{0,1:T(8,128)(2,1)}), bf16[512,512]{0,1:T(8,128)(2,1)}) %all-reduce.5.cloned.1.call-update) | async-done | bytes 524304 | tf_op jit(solution)/shard_map/psum | solution.py:111
  778.2 2.2 copy.21
  780.4 32.0 %reduce-scatter.15.cloned.1.call-done = bf16[64,16]{1,0:T(8,128)(2,1)} async-done(((bf16[512,16]{1,0:T(8,128)(2,1)}), bf16[64,16]{1,0:T(8,128)(2,1)}) %reduce-scatter.15.cloned.1.call-update) | async-done | bytes 2064
  812.4 0.8 copy.29
  813.2 0.6 convert_element_type.365
  813.8 33.0 %reduce-scatter.13.cloned.1.call-done = bf16[128,16]{1,0:T(8,128)(2,1)} async-done(((bf16[1024,16]{1,0:T(8,128)(2,1)}), bf16[128,16]{1,0:T(8,128)(2,1)}) %reduce-scatter.13.cloned.1.call-update) | async-done | bytes 4112
  846.8 0.8 copy.27
  847.6 0.6 convert_element_type.363
  848.3 247.1 %all-reduce.7.cloned.1.call-done = (f32[31,512]{1,0:T(8,128)}, f32[8,512]{1,0:T(8,128)}) async-done(((f32[31,512]{1,0:T(8,128)}, f32[8,512]{1,0:T(8,128)}), (f32[31,512]{1,0:T(8,128)}, f32[8,512]{1,0:T(8,128)})) %all-reduce.7.cloned.1.call-update) | async-done | bytes 79888 | tf_op jit(solution)/shard_map/psum | solution.py:109
  1095.4 1.5 copy.45
  1096.9 1.3 copy.46
  (207 shorter events, 2.5 us)
Async XLA Ops:
  7.2 4.2 copy-start
  7.2 4.2 copy-start.5
  7.2 483.4 %reduce-scatter.11.cloned.1.call-start = ((), (), s32[]{:S(2)}) async-start(), calls=%async_computation.5 | async-start | bytes 540672 | tf_op jit(solution)/shard_map/reduce_scatter | solution.py:97
  12.4 6.8 copy-start.13
  12.4 7.2 copy-start.11
  14.0 6.7 collective-permute-start
  17.9 4.5 collective-permute-start.1
  19.2 3.1 copy-start.18
  19.3 3.1 copy-start.20
  19.3 3.1 copy-start.28
  19.3 3.1 copy-start.30
  19.3 3.1 copy-start.32
  19.3 3.1 copy-start.34
  19.3 3.1 copy-start.36
  19.3 12.7 %copy-start.22 = (f32[1,512]{1,0:T(1,128)}, f32[1,512]{1,0:T(1,128)S(1)}, u32[]{:S(2)}) copy-start(f32[1,512]{1,0:T(1,128)S(1)} %get-tuple-element.89) | copy-start | bytes 6148
  19.3 12.7 %copy-start.24 = (f32[1,512]{1,0:T(1,128)}, f32[1,512]{1,0:T(1,128)S(1)}, u32[]{:S(2)}) copy-start(f32[1,512]{1,0:T(1,128)S(1)} %get-tuple-element.90) | copy-start | bytes 6148
  19.4 12.7 %copy-start.26 = (f32[1,512]{1,0:T(1,128)}, f32[1,512]{1,0:T(1,128)S(1)}, u32[]{:S(2)}) copy-start(f32[1,512]{1,0:T(1,128)S(1)} %get-tuple-element.91) | copy-start | bytes 6148
  20.6 11.5 %copy-start.6 = (bf16[1,704,512]{2,1,0:T(8,128)(2,1)S(1)}, bf16[1,704,512]{2,1,0:T(8,128)(2,1)}, u32[]{:S(2)}) copy-start(bf16[1,704,512]{2,1,0:T(8,128)(2,1)} %param.9) | copy-start | bytes 2162692
  20.6 11.5 %copy-start.90 = (bf16[512,512]{1,0:T(8,128)(2,1)S(1)}, bf16[512,512]{1,0:T(8,128)(2,1)}, u32[]{:S(2)}) copy-start(bf16[512,512]{1,0:T(8,128)(2,1)} %param.13) | copy-start | bytes 1572868
  34.1 181.2 %copy-start.10 = (bf16[256,512]{1,0:T(8,128)(2,1)S(1)}, bf16[256,512]{1,0:T(8,128)(2,1)}, u32[]{:S(2)}) copy-start(bf16[256,512]{1,0:T(8,128)(2,1)} %param.16) | copy-start | bytes 786436
  209.5 11.7 %copy-start.12 = (f32[1,8,512]{2,1,0:T(8,128)S(1)}, f32[1,8,512]{2,1,0:T(8,128)}, u32[]{:S(2)}) copy-start(f32[1,8,512]{2,1,0:T(8,128)} %get-tuple-element.60) | copy-start | bytes 49156
  222.1 4.1 copy-start.17
  230.8 7.3 collective-permute-start.2
  232.0 6.0 copy-start.15
  232.1 6.0 copy-start.19
  232.1 6.0 copy-start.21
  232.1 6.0 copy-start.23
  232.1 6.0 copy-start.25
  232.1 6.0 copy-start.27
  232.1 6.0 copy-start.29
  232.1 6.0 copy-start.31
  232.1 6.0 copy-start.33
  232.1 6.0 copy-start.35
  232.1 6.0 copy-start.37
  232.2 6.0 copy-start.39
  232.2 6.0 copy-start.41
  232.2 6.0 copy-start.43
  232.2 6.0 copy-start.45
  232.2 6.0 copy-start.47
  232.2 6.0 copy-start.49
  232.2 6.0 copy-start.51
  232.2 6.0 copy-start.53
  232.2 6.0 copy-start.55
  232.2 6.0 copy-start.57
  232.3 6.0 copy-start.59
  232.3 6.0 copy-start.61
  232.3 6.0 copy-start.63
  232.3 6.0 copy-start.65
  232.3 6.0 copy-start.67
  232.3 6.0 copy-start.69
  232.3 6.0 copy-start.71
  232.3 6.0 copy-start.73
  232.3 6.0 copy-start.75
  232.3 6.0 copy-start.77
  232.4 6.0 copy-start.79
  232.4 5.7 collective-permute-start.3
  238.0 470.2 %reduce-scatter.9.cloned.1.call-start = ((), (), s32[]{:S(2)}) async-start(), calls=%async_computation.4 | async-start | bytes 1081344 | tf_op jit(solution)/shard_map/reduce_scatter | solution.py:94
  238.1 26.0 %copy-start.4 = (f32[1,704,1024]{2,1,0:T(8,128)S(1)}, f32[1,704,1024]{2,1,0:T(8,128)}, u32[]{:S(2)}) copy-start(f32[1,704,1024]{2,1,0:T(8,128)} %copy-done.3) | copy-start | bytes 8650756
  267.4 510.9 %all-reduce.5.cloned.1.call-start = ((), (), s32[]{:S(2)}) async-start(), calls=%async_computation.6 | async-start | bytes 1048576 | tf_op jit(solution)/shard_map/psum | solution.py:111
  268.5 544.0 %reduce-scatter.15.cloned.1.call-start = ((), (), s32[]{:S(2)}) async-start(), calls=%async_computation.8 | async-start | bytes 147456
  492.1 354.7 %reduce-scatter.13.cloned.1.call-start = ((), (), s32[]{:S(2)}) async-start(), calls=%async_computation.7 | async-start | bytes 294912
  494.4 219.4 %copy-start.84 = (f32[256]{0:T(256)S(1)}, f32[256]{0:T(256)}, u32[]{:S(2)}) copy-start(f32[256]{0:T(256)} %copy-done.83) | copy-start | bytes 3076
  494.4 219.4 %copy-start.87 = (f32[1,256]{1,0:T(1,128)S(1)}, f32[1,256]{1,0:T(1,128)}, u32[]{:S(2)}) copy-start(f32[1,256]{1,0:T(1,128)} %param.17) | copy-start | bytes 3076
  709.8 385.6 %all-reduce.7.cloned.1.call-start = ((), (), s32[]{:S(2)}) async-start(), calls=%async_computation.9 | async-start | bytes 163840 | tf_op jit(solution)/shard_map/psum | solution.py:109
  (38 other events, 84.5 us)
Sparse Core Ops, SparseCore 0:
  238.1 252.4 reduce-scatter.10
  495.5 212.6 reduce-scatter.8
  710.6 67.5 all-reduce.4
  780.6 31.8 reduce-scatter.14
  814.9 31.8 reduce-scatter.12
  852.8 242.5 all-reduce.6
where the time goes:
time: 1110 us
  waiting for transfers between devices  788 us (71%)
  blocking collectives  192 us (17%)
  other arithmetic  55.3 us (5%)
  between operations  20.1 us (2%)
  matrix products  20 us (2%)
  local copies, waits for them, and re-layouts  19.4 us (2%)
    psum x1, waiting for transfers between devices, shards(): grad_kernel, grad_query = lax.psum((kernel_here, query_here), ('ep', 'seq'))  247 us
    reduce_scatter x1, waiting for transfers between devices, shards(): lax.psum_scatter(out_here.astype(jnp.bfloat16), 'seq', scatter_dimension=...  216 us
    reduce_scatter x1, waiting for transfers between devices, shards(): lax.psum_scatter(in_here.astype(jnp.bfloat16), 'seq', scatter_dimension=0...  214 us
    psum x1, blocking collectives, shards(): total, vec = lax.psum((jnp.sum(expo, axis=1), vec_here), 'seq')  111 us
    unnamed x8, waiting for transfers between devices  65.1 us
    pmax x1, blocking collectives, shards(): top = lax.pmax(jnp.max(masked, axis=1), 'seq')  62.9 us
    psum x1, waiting for transfers between devices, shards(): lax.psum(value_here.astype(jnp.bfloat16), 'ep').astype(jnp.float32)  44.1 us
    concatenate x2, other arithmetic, shards(): jnp.concatenate([dglu * sig, dglu * mixed[..., :width] * sig * (1.0 - sig...  26.3 us
  transfers between devices with their start and end apart: 10, of which 7 were waited for; matrix products, arithmetic and copies ran while one was open for 5% of the time, Pallas kernels for 0%

commit v1 on v0

--- a/solution.py
+++ b/solution.py
@@ -108,7 +108,7 @@
     )
     grad_kernel, grad_query = lax.psum((kernel_here, query_here), ("ep", "seq"))
     grad_value, loss = (
-        lax.psum(value_here.astype(jnp.bfloat16), "ep").astype(jnp.float32),
+        jnp.sum(lax.all_gather(value_here.astype(jnp.bfloat16), "ep"), axis=0).astype(jnp.float32),
         lax.psum(loss_here.astype(jnp.bfloat16), "ep").astype(jnp.float32),
     )
     return (loss, grad_in, grad_out, grad_kernel, grad_query, grad_value)

time: 1110 us -> 981 us (0.88)
  waiting for transfers between devices: 788 us -> 659 us
    psum x1, waiting for transfers between devices: 247 us -> 146 us  [shards(): grad_kernel, grad_query = lax.psum((kernel_here, query_here), ('ep', 'seq'))]
    psum x1 -> x0, waiting for transfers between devices: 44.1 us -> none  [shards(): lax.psum(value_here.astype(jnp.bfloat16), 'ep').astype(jnp.float32)]
    all_gather x0 -> x1, waiting for transfers between devices: none -> 36.9 us  [shards(): lax.all_gather(value_here.astype(jnp.bfloat16), 'ep')]
    unnamed x8, waiting for transfers between devices: 65.1 us -> 34.8 us
  transfers between devices with their start and end apart: 10 -> 10, of which waited for: 7 -> 7; matrix products, arithmetic and copies ran while one was open for 5% -> 6% of each run, Pallas kernels for 0% -> 0%
where the time goes in v1:
time: 981 us; the launch traced here: 980 us
  waiting for transfers between devices  659 us (67%)
  blocking collectives  191 us (19%)
  other arithmetic  58.8 us (6%)
  between operations  21.3 us (2%)
  matrix products  19.9 us (2%)
  local copies, waits for them, and re-layouts  19.1 us (2%)
  starting transfers between devices  10.9 us (1%)
    reduce_scatter x1, waiting for transfers between devices, shards(): lax.psum_scatter(out_here.astype(jnp.bfloat16), 'seq', scatter_dimension=...  224 us
    reduce_scatter x1, waiting for transfers between devices, shards(): lax.psum_scatter(in_here.astype(jnp.bfloat16), 'seq', scatter_dimension=0...  216 us
    psum x1, waiting for transfers between devices, shards(): grad_kernel, grad_query = lax.psum((kernel_here, query_here), ('ep', 'seq'))  146 us
    psum x1, blocking collectives, shards(): total, vec = lax.psum((jnp.sum(expo, axis=1), vec_here), 'seq')  110 us
    pmax x1, blocking collectives, shards(): top = lax.pmax(jnp.max(masked, axis=1), 'seq')  62.9 us
    all_gather x1, waiting for transfers between devices, shards(): lax.all_gather(value_here.astype(jnp.bfloat16), 'ep')  36.9 us
    unnamed x8, waiting for transfers between devices  34.8 us
    concatenate x2, other arithmetic, shards(): jnp.concatenate([dglu * sig, dglu * mixed[..., :width] * sig * (1.0 - sig...  26.8 us
  transfers between devices with their start and end apart: 10, of which 7 were waited for; matrix products, arithmetic and copies ran while one was open for 6% of the time, Pallas kernels for 0%

profile of v1, /device:TPU:1, one launch (start us, length us, event | category | flops | bytes accessed | tf_op | source)
XLA Modules:
  0.0 980.2 jit_solution(1881273549521119915)
XLA Ops:
  8.8 1.3 convert_reduce_fusion
  10.2 1.5 fusion.5
  12.2 1.0 convolution_bitcast_fusion
  13.7 1.1 copy-done.3
  14.8 3.9 collective-permute-start
  18.7 1.3 collective-permute-start.1
  20.5 1.0 copy.20
  21.5 1.8 collective-permute-done.1
  23.2 9.3 fusion.36
  32.9 0.6 fusion.37
  34.0 0.9 fusion.189
  34.8 62.9 %pmax.7 = f32[8]{0:T(128)S(1)} all-reduce(f32[8]{0:T(128)S(1)} %get-tuple-element.83), channel_id=1, replica_groups=mesh['ep'=8,'seq'=32] {'seq'}, use_global_device_ids=true, to_apply=%region_3.4 | all-reduce | flops 8 | bytes 64 | tf_op jit(solution)/shard_map/pmax | solution.py:49
  97.7 0.7 fusion.164
  98.4 0.8 convolution_bitcast_fusion.3
  99.2 110.2 %all-reduce.1 = (f32[1,8,512]{2,1,0:T(8,128)}, f32[8]{0:T(128)S(1)}) all-reduce(f32[1,8,512]{2,1,0:T(8,128)S(1)} %convolution_bitcast_fusion.3, f32[8]{0:T(128)} %fusion.164), channel_id=1, replica_groups=mesh['ep'=8,'seq'=32] {'seq'}, use_global_device_ids=true, to_apply=%region_4.5 | all-reduce | flops 4104 | bytes 32832 | tf_op jit(solution)/shard_map/psum | solution.py:52
  209.5 0.9 fusion.180
  210.3 1.5 fusion.161
  211.9 0.6 multiply_reduce_fusion
  213.2 0.7 broadcast_divide_fusion.1
  213.9 0.6 div.113
  214.5 0.7 reshape.308
  215.2 1.0 fusion.190
  216.2 0.9 fusion.171
  217.1 1.3 multiply_reduce_fusion.1
  219.0 0.6 subtract_divide_fusion
  219.7 1.4 fusion.191
  221.1 0.8 fusion.181
  221.9 2.1 fusion.159
  224.0 1.9 fusion.94
  226.0 0.8 fusion.93
  227.4 2.2 fusion.67
  229.6 0.9 copy-done.1
  230.4 1.3 collective-permute-start.2
  232.0 4.2 collective-permute-start.3
  236.2 1.5 convolution_convert_fusion.1
  238.1 26.2 %fusion.96 = (bf16[704,512]{1,0:T(8,128)(2,1)S(1)}, f32[1,704,512]{2,1,0:T(8,128)S(1)}) fusion(f32[1,704,1024]{2,1,0:T(8,128)} %copy-done.3, f32[704]{0:T(1024)S(1)} %copy-done.15, bf16[1,704,512]{2,1,0:T(8,128)(2,1)} %copy-done.1, bf16[1,15,512]{2,1,0:T(8,128)(2,1)S(1)} %collective-permute-done.3, f32[512]{0:T(512)S(1)} %bitcast.173, f32[512]{0:T(512)S(1)} %bitcast.175, ...), kind=kLoop, calls=%fused_computation.235 | loop fusion | flops 67764224 | bytes 4422400 | tf_op jit(solution)/shard_map/concatenate | solution.py:89
  264.3 0.6 fusion.97
  265.4 2.1 convolution_convert_fusion
  267.6 223.6 %reduce-scatter.11.cloned.1.call-done = bf16[16,512]{1,0:T(8,128)(2,1)} async-done(((bf16[512,512]{1,0:T(8,128)(2,1)}), bf16[16,512]{1,0:T(8,128)(2,1)}) %reduce-scatter.11.cloned.1.call-update) | async-done | bytes 16400 | tf_op jit(solution)/shard_map/reduce_scatter | solution.py:97
  491.2 1.5 copy.28
  492.8 215.7 %reduce-scatter.9.cloned.1.call-done = bf16[16,1024]{1,0:T(8,128)(2,1)} async-done(((bf16[512,1024]{1,0:T(8,128)(2,1)}), bf16[16,1024]{1,0:T(8,128)(2,1)}) %reduce-scatter.9.cloned.1.call-update) | async-done | bytes 32784 | tf_op jit(solution)/shard_map/reduce_scatter | solution.py:94
  708.5 1.6 copy.26
  710.2 0.9 multiply_convert_fusion.4
  711.1 2.0 copy.21
  713.3 2.3 fusion.68
  715.6 1.5 fusion.82
  717.1 1.5 fusion.83
  718.6 1.7 fusion.84
  720.3 2.5 stack.127
  722.8 1.4 convolution_multiply_fusion.2
  724.3 0.6 multiply_reduce_fusion.2
  725.5 18.3 %psum.37 = bf16[]{:T(256)} all-reduce(bf16[]{:T(256)S(6)} %div.117), channel_id=1, replica_groups=mesh['ep'=8,'seq'=32] {'ep'}, use_global_device_ids=true, to_apply=%region_9.10 | all-reduce | flops 1 | bytes 4 | tf_op jit(solution)/shard_map/psum | solution.py:112
  744.5 1.0 reduce-scatter.15.cloned.1.call-done
  745.5 0.8 copy.29
  746.3 0.6 convert_element_type.374
  746.9 33.7 %reduce-scatter.13.cloned.1.call-done = bf16[128,16]{1,0:T(8,128)(2,1)} async-done(((bf16[1024,16]{1,0:T(8,128)(2,1)}), bf16[128,16]{1,0:T(8,128)(2,1)}) %reduce-scatter.13.cloned.1.call-update) | async-done | bytes 4112
  780.6 0.8 copy.27
  781.4 0.6 convert_element_type.372
  782.0 36.9 %all-gather.2.cloned.1.call-done = bf16[8,512,512]{2,1,0:T(8,128)(2,1)} async-done(((bf16[1,512,512]{2,1,0:T(8,128)(2,1)}), bf16[8,512,512]{2,1,0:T(8,128)(2,1)}) %all-gather.2.cloned.1.call-update) | async-done | bytes 4194320 | tf_op jit(solution)/shard_map/all_gather | solution.py:111
  819.0 3.1 reduce_sum.395
  822.0 1.1 convert_element_type.378
  823.2 146.0 %all-reduce.4.cloned.1.call-done = (f32[31,512]{1,0:T(8,128)}, f32[8,512]{1,0:T(8,128)}) async-done(((f32[31,512]{1,0:T(8,128)}, f32[8,512]{1,0:T(8,128)}), (f32[31,512]{1,0:T(8,128)}, f32[8,512]{1,0:T(8,128)})) %all-reduce.4.cloned.1.call-update) | async-done | bytes 79888 | tf_op jit(solution)/shard_map/psum | solution.py:109
  969.1 1.5 copy.44
  970.6 1.3 copy.45
  (209 shorter events, 3.6 us)
Async XLA Ops:
  8.0 483.2 %reduce-scatter.11.cloned.1.call-start = ((), (), s32[]{:S(2)}) async-start(), calls=%async_computation.5 | async-start | bytes 540672 | tf_op jit(solution)/shard_map/reduce_scatter | solution.py:97
  13.2 6.8 copy-start.13
  13.2 7.2 copy-start.11
  14.8 6.7 collective-permute-start
  18.7 4.5 collective-permute-start.1
  20.1 12.5 %copy-start.22 = (f32[1,512]{1,0:T(1,128)}, f32[1,512]{1,0:T(1,128)S(1)}, u32[]{:S(2)}) copy-start(f32[1,512]{1,0:T(1,128)S(1)} %get-tuple-element.71) | copy-start | bytes 6148
  20.1 12.5 %copy-start.24 = (f32[1,512]{1,0:T(1,128)}, f32[1,512]{1,0:T(1,128)S(1)}, u32[]{:S(2)}) copy-start(f32[1,512]{1,0:T(1,128)S(1)} %get-tuple-element.72) | copy-start | bytes 6148
  20.1 12.5 %copy-start.26 = (f32[1,512]{1,0:T(1,128)}, f32[1,512]{1,0:T(1,128)S(1)}, u32[]{:S(2)}) copy-start(f32[1,512]{1,0:T(1,128)S(1)} %get-tuple-element.73) | copy-start | bytes 6148
  20.1 12.5 %copy-start.28 = (f32[1,512]{1,0:T(1,128)}, f32[1,512]{1,0:T(1,128)S(1)}, u32[]{:S(2)}) copy-start(f32[1,512]{1,0:T(1,128)S(1)} %get-tuple-element.74) | copy-start | bytes 6148
  20.1 12.5 %copy-start.30 = (f32[1,512]{1,0:T(1,128)}, f32[1,512]{1,0:T(1,128)S(1)}, u32[]{:S(2)}) copy-start(f32[1,512]{1,0:T(1,128)S(1)} %get-tuple-element.75) | copy-start | bytes 6148
  20.1 12.5 %copy-start.32 = (f32[1,512]{1,0:T(1,128)}, f32[1,512]{1,0:T(1,128)S(1)}, u32[]{:S(2)}) copy-start(f32[1,512]{1,0:T(1,128)S(1)} %get-tuple-element.76) | copy-start | bytes 6148
  20.2 12.5 %copy-start.34 = (f32[1,512]{1,0:T(1,128)}, f32[1,512]{1,0:T(1,128)S(1)}, u32[]{:S(2)}) copy-start(f32[1,512]{1,0:T(1,128)S(1)} %get-tuple-element.77) | copy-start | bytes 6148
  20.2 12.5 %copy-start.36 = (f32[1,512]{1,0:T(1,128)}, f32[1,512]{1,0:T(1,128)S(1)}, u32[]{:S(2)}) copy-start(f32[1,512]{1,0:T(1,128)S(1)} %get-tuple-element.78) | copy-start | bytes 6148
  20.2 12.5 %copy-start.38 = (f32[1,512]{1,0:T(1,128)}, f32[1,512]{1,0:T(1,128)S(1)}, u32[]{:S(2)}) copy-start(f32[1,512]{1,0:T(1,128)S(1)} %get-tuple-element.79) | copy-start | bytes 6148
  20.2 12.5 %copy-start.40 = (f32[1,512]{1,0:T(1,128)}, f32[1,512]{1,0:T(1,128)S(1)}, u32[]{:S(2)}) copy-start(f32[1,512]{1,0:T(1,128)S(1)} %get-tuple-element.80) | copy-start | bytes 6148
  20.2 12.4 %copy-start.42 = (f32[1,512]{1,0:T(1,128)}, f32[1,512]{1,0:T(1,128)S(1)}, u32[]{:S(2)}) copy-start(f32[1,512]{1,0:T(1,128)S(1)} %get-tuple-element.50) | copy-start | bytes 6148
  20.2 12.4 %copy-start.44 = (f32[1,512]{1,0:T(1,128)}, f32[1,512]{1,0:T(1,128)S(1)}, u32[]{:S(2)}) copy-start(f32[1,512]{1,0:T(1,128)S(1)} %get-tuple-element.51) | copy-start | bytes 6148
  20.3 12.4 %copy-start.46 = (f32[1,512]{1,0:T(1,128)}, f32[1,512]{1,0:T(1,128)S(1)}, u32[]{:S(2)}) copy-start(f32[1,512]{1,0:T(1,128)S(1)} %get-tuple-element.52) | copy-start | bytes 6148
  20.3 12.4 %copy-start.48 = (f32[1,512]{1,0:T(1,128)}, f32[1,512]{1,0:T(1,128)S(1)}, u32[]{:S(2)}) copy-start(f32[1,512]{1,0:T(1,128)S(1)} %get-tuple-element.53) | copy-start | bytes 6148
  20.3 12.4 %copy-start.50 = (f32[1,512]{1,0:T(1,128)}, f32[1,512]{1,0:T(1,128)S(1)}, u32[]{:S(2)}) copy-start(f32[1,512]{1,0:T(1,128)S(1)} %get-tuple-element.54) | copy-start | bytes 6148
  20.3 12.4 %copy-start.52 = (f32[1,512]{1,0:T(1,128)}, f32[1,512]{1,0:T(1,128)S(1)}, u32[]{:S(2)}) copy-start(f32[1,512]{1,0:T(1,128)S(1)} %get-tuple-element.55) | copy-start | bytes 6148
  20.3 12.4 %copy-start.54 = (f32[1,512]{1,0:T(1,128)}, f32[1,512]{1,0:T(1,128)S(1)}, u32[]{:S(2)}) copy-start(f32[1,512]{1,0:T(1,128)S(1)} %get-tuple-element.56) | copy-start | bytes 6148
  20.3 12.4 %copy-start.56 = (f32[1,512]{1,0:T(1,128)}, f32[1,512]{1,0:T(1,128)S(1)}, u32[]{:S(2)}) copy-start(f32[1,512]{1,0:T(1,128)S(1)} %get-tuple-element.57) | copy-start | bytes 6148
  20.3 12.4 %copy-start.58 = (f32[1,512]{1,0:T(1,128)}, f32[1,512]{1,0:T(1,128)S(1)}, u32[]{:S(2)}) copy-start(f32[1,512]{1,0:T(1,128)S(1)} %get-tuple-element.58) | copy-start | bytes 6148
  20.3 12.4 %copy-start.60 = (f32[1,512]{1,0:T(1,128)}, f32[1,512]{1,0:T(1,128)S(1)}, u32[]{:S(2)}) copy-start(f32[1,512]{1,0:T(1,128)S(1)} %get-tuple-element.59) | copy-start | bytes 6148
  20.3 12.4 %copy-start.62 = (f32[1,512]{1,0:T(1,128)}, f32[1,512]{1,0:T(1,128)S(1)}, u32[]{:S(2)}) copy-start(f32[1,512]{1,0:T(1,128)S(1)} %get-tuple-element.60) | copy-start | bytes 6148
  20.3 12.4 %copy-start.64 = (f32[1,512]{1,0:T(1,128)}, f32[1,512]{1,0:T(1,128)S(1)}, u32[]{:S(2)}) copy-start(f32[1,512]{1,0:T(1,128)S(1)} %get-tuple-element.61) | copy-start | bytes 6148
  20.4 12.4 %copy-start.66 = (f32[1,512]{1,0:T(1,128)}, f32[1,512]{1,0:T(1,128)S(1)}, u32[]{:S(2)}) copy-start(f32[1,512]{1,0:T(1,128)S(1)} %get-tuple-element.62) | copy-start | bytes 6148
  20.4 12.4 %copy-start.68 = (f32[1,512]{1,0:T(1,128)}, f32[1,512]{1,0:T(1,128)S(1)}, u32[]{:S(2)}) copy-start(f32[1,512]{1,0:T(1,128)S(1)} %get-tuple-element.63) | copy-start | bytes 6148
  20.4 12.4 %copy-start.70 = (f32[1,512]{1,0:T(1,128)}, f32[1,512]{1,0:T(1,128)S(1)}, u32[]{:S(2)}) copy-start(f32[1,512]{1,0:T(1,128)S(1)} %get-tuple-element.64) | copy-start | bytes 6148
  20.4 12.4 %copy-start.72 = (f32[1,512]{1,0:T(1,128)}, f32[1,512]{1,0:T(1,128)S(1)}, u32[]{:S(2)}) copy-start(f32[1,512]{1,0:T(1,128)S(1)} %get-tuple-element.65) | copy-start | bytes 6148
  20.4 12.4 %copy-start.74 = (f32[1,512]{1,0:T(1,128)}, f32[1,512]{1,0:T(1,128)S(1)}, u32[]{:S(2)}) copy-start(f32[1,512]{1,0:T(1,128)S(1)} %get-tuple-element.66) | copy-start | bytes 6148
  20.4 12.4 %copy-start.76 = (f32[1,512]{1,0:T(1,128)}, f32[1,512]{1,0:T(1,128)S(1)}, u32[]{:S(2)}) copy-start(f32[1,512]{1,0:T(1,128)S(1)} %get-tuple-element.67) | copy-start | bytes 6148
  20.4 12.4 %copy-start.78 = (f32[1,512]{1,0:T(1,128)}, f32[1,512]{1,0:T(1,128)S(1)}, u32[]{:S(2)}) copy-start(f32[1,512]{1,0:T(1,128)S(1)} %get-tuple-element.68) | copy-start | bytes 6148
  21.5 11.4 %copy-start.6 = (bf16[1,704,512]{2,1,0:T(8,128)(2,1)S(1)}, bf16[1,704,512]{2,1,0:T(8,128)(2,1)}, u32[]{:S(2)}) copy-start(bf16[1,704,512]{2,1,0:T(8,128)(2,1)} %param.9) | copy-start | bytes 2162692
  21.5 11.4 %copy-start.90 = (bf16[512,512]{1,0:T(8,128)(2,1)S(1)}, bf16[512,512]{1,0:T(8,128)(2,1)}, u32[]{:S(2)}) copy-start(bf16[512,512]{1,0:T(8,128)(2,1)} %param.13) | copy-start | bytes 1572868
  34.8 180.3 %copy-start.10 = (bf16[256,512]{1,0:T(8,128)(2,1)S(1)}, bf16[256,512]{1,0:T(8,128)(2,1)}, u32[]{:S(2)}) copy-start(bf16[256,512]{1,0:T(8,128)(2,1)} %param.16) | copy-start | bytes 786436
  209.5 11.6 %copy-start.12 = (f32[1,8,512]{2,1,0:T(8,128)S(1)}, f32[1,8,512]{2,1,0:T(8,128)}, u32[]{:S(2)}) copy-start(f32[1,8,512]{2,1,0:T(8,128)} %get-tuple-element.42) | copy-start | bytes 49156
  230.4 7.3 collective-permute-start.2
  231.7 6.1 copy-start.15
  231.7 6.1 copy-start.19
  231.7 6.1 copy-start.21
  231.8 6.1 copy-start.23
  231.8 6.1 copy-start.25
  231.8 6.1 copy-start.27
  231.8 6.1 copy-start.29
  231.8 6.1 copy-start.31
  231.8 6.1 copy-start.33
  231.8 6.1 copy-start.35
  231.8 6.1 copy-start.37
  231.8 6.1 copy-start.39
  231.8 6.1 copy-start.41
  231.9 6.1 copy-start.43
  231.9 6.1 copy-start.45
  231.9 6.1 copy-start.47
  231.9 6.1 copy-start.49
  231.9 6.1 copy-start.51
  232.0 5.7 collective-permute-start.3
  237.7 470.8 %reduce-scatter.9.cloned.1.call-start = ((), (), s32[]{:S(2)}) async-start(), calls=%async_computation.4 | async-start | bytes 1081344 | tf_op jit(solution)/shard_map/reduce_scatter | solution.py:94
  237.8 26.5 %copy-start.4 = (f32[1,704,1024]{2,1,0:T(8,128)S(1)}, f32[1,704,1024]{2,1,0:T(8,128)}, u32[]{:S(2)}) copy-start(f32[1,704,1024]{2,1,0:T(8,128)} %copy-done.3) | copy-start | bytes 8650756
  267.6 478.0 %reduce-scatter.15.cloned.1.call-start = ((), (), s32[]{:S(2)}) async-start(), calls=%async_computation.8 | async-start | bytes 147456
  492.7 287.9 %reduce-scatter.13.cloned.1.call-start = ((), (), s32[]{:S(2)}) async-start(), calls=%async_computation.7 | async-start | bytes 294912
  710.2 108.8 %all-gather.2.cloned.1.call-start = ((), (), s32[]{:S(2)}) async-start(), calls=%async_computation.6 | async-start | bytes 4718592 | tf_op jit(solution)/shard_map/all_gather | solution.py:111
  713.2 255.9 %all-reduce.4.cloned.1.call-start = ((), (), s32[]{:S(2)}) async-start(), calls=%async_computation.9 | async-start | bytes 163840 | tf_op jit(solution)/shard_map/psum | solution.py:109
  (38 other events, 135.0 us)
Sparse Core Ops, SparseCore 0:
  237.8 253.3 reduce-scatter.10
  496.1 212.4 reduce-scatter.8
  711.2 34.3 reduce-scatter.14
  747.9 32.6 reduce-scatter.12
  782.5 36.4 all-gather.1
Sparse Core Ops, SparseCore 1:
  724.3 244.7 all-reduce.3
